TPU v7x, 32 devices: a whole 2x2x4 slice. The times are simulated.
32 devices in a mesh: slab: 8 (over z, y), disk: 4 (over x, core).
Axes of the slice: x: 2, y: 2, z: 4, core: 2. Of those that a mesh axis runs over, the one named last changes fastest.
Arguments:
- thermal_anomaly: float32 [2, 8, 1024], P(None, 'slab', 'disk'), may hold values from 0.5 to 1.5
- humidity_amount: float32 [2, 8, 1024], P(None, 'slab', 'disk'), may hold values from 0.2 to 2
- slab_condensate_amount: float32 [2, 8, 1024], P(None, 'slab', 'disk'), may hold values from 0.1 to 2
- overcast_indicator: int32 [2, 1024], P(None, 'disk'), may hold values 0 or 1
- molecular_opacity: float32 [112, 8], replicated, may hold values from 0.003 to 0.1
- condensate_opacity: float32 [112], replicated, may hold values from 0.01 to 0.1
- planck_quadrature_factor: float32 [112], replicated, may hold values from 0.5 to 2
- scene_contributing_profiles: int32 [4, 16384], P(None, ('slab', 'disk')), may hold values from 0 to 1023, as said below
- scene_interpolation_factors: float32 [4, 16384], P(None, ('slab', 'disk')), may hold values from 0.1 to 1
Outputs:
- pixel_radiance: float32 [2, 16, 16384], P(None, None, ('slab', 'disk'))
Inputs may be any that keep to these rules, and one draw needn't show every extreme that they name: `scene_contributing_profiles`: every source column c of pixel p lies in the pixel's latitude strip: (c % 256) // 32 == p // 2048.
All inputs are finite; a program needn't handle non-finite values. No bound on the sum of `overcast_indicator` on one device may be relied on, other than what follows from the above.
Results may differ from a plain program's by a relative error of at most 0.0017.
Values may be sent and summed in bfloat16 or wider, within the bound.
A program may use at most 64 MiB of HBM per device.

v0:
```python
import functools

import jax
import jax.numpy as jnp
from jax import lax
from jax.experimental import pallas as pl
from jax.experimental.pallas import tpu as pltpu
from jax.sharding import PartitionSpec as P

BANDS = 16
GPB = 7
LANES = 128
MESH = pl.DeviceIdType.MESH
NEG_LOG2E = -1.4426950408889634


def split(x):
    hi = x.astype(jnp.bfloat16).astype(jnp.float32)
    return hi, x - hi


def div(x, by):
    return x >> (by.bit_length() - 1) if by & (by - 1) == 0 else lax.div(x, by)


def rem(x, by):
    return x & (by - 1) if by & (by - 1) == 0 else lax.rem(x, by)


def kernel(
    n_slab, n_disk, sector_cols, block_cols,
    t_ref, q_ref, c_ref, o_ref, mol_ref, cond_ref, pf_ref, src_ref, w_ref,
    out_ref,
    fld, pk, recv, cmat, mmat, amat, fmat, zmat, bmat, smat, whi, wlo,
    send_sem, recv_sem,
):
    n = n_slab * n_disk
    levels = n_slab
    gs = BANDS * GPB
    halves = sector_cols // LANES
    per = LANES // block_cols
    me_s = lax.axis_index("slab")
    me_d = lax.axis_index("disk")
    me = me_s * n_disk + me_d

    def partner(i):
        return me ^ (n - 1 - i) if n & (n - 1) == 0 else rem(me + (i + 1), n)

    barrier = pltpu.get_barrier_semaphore()

    def greet(i, carry):
        peer = partner(i)
        pl.semaphore_signal(
            barrier, inc=1, device_id=(div(peer, n_disk), rem(peer, n_disk)), device_id_type=MESH
        )
        return carry

    lax.fori_loop(0, n - 1, greet, 0)

    for h in range(2):
        for k in range(halves):
            cols = pl.ds(k * LANES, LANES)
            cloud = jnp.where(o_ref[h:h + 1, cols] == 1, c_ref[h, :, cols], 0.0)
            t2 = t_ref[h, :, cols] * t_ref[h, :, cols]
            vapour = q_ref[h, :, cols]
            fld[h, pl.ds(2 * k, 1), :] = t2 * t2
            fld[h, pl.ds(2 * k + 1, 1), :] = cloud
            fld[h, pl.ds(2 * (halves + k), 1), :] = vapour
            fld[h, pl.ds(2 * (halves + k) + 1, 1), :] = vapour
    rows = 4 * halves
    lane = lax.broadcasted_iota(jnp.int32, (rows, LANES), 1)
    first_hour = (lane & block_cols) == 0
    odd = rem(me_d, 2)
    turn = odd * (2 * block_cols)
    own = div(lane[:rows // 2], 2 * block_cols) == odd
    f0 = pltpu.roll(fld[0], turn, 1)
    f1 = pltpu.roll(fld[1], turn, 1)
    for s in range(per):
        x = pltpu.roll(f0, (LANES - s * block_cols) % LANES, 1) if s else f0
        y = pltpu.roll(f1, (LANES + block_cols - s * block_cols) % LANES, 1) if s != 1 else f1
        p = jnp.where(first_hour, x, y)
        p = jnp.where(own, p[:rows // 2], pltpu.roll(p[rows // 2:], LANES // 2, 1))
        for k in range(halves):
            pk[k * per + s] = p[2 * k:2 * k + 2, :]

    mol_hi, mol_lo = split(jnp.transpose(mol_ref[...]) * NEG_LOG2E)
    cond_hi, cond_lo = split(cond_ref[...] * NEG_LOG2E)
    cmat[...] = jnp.zeros_like(cmat)
    for at, part in enumerate((mol_hi, cond_hi, mol_lo, cond_lo, mol_hi, cond_hi)):
        cmat[pl.ds(at * levels, levels), pl.ds(0, gs)] = jnp.broadcast_to(part, (levels, gs))
    mmat[...] = jnp.transpose(cmat[...])
    col = rem(lax.broadcasted_iota(jnp.int32, (gs, 6 * levels), 1), levels)

    def upto(l):
        return jnp.where(col <= l, mmat[pl.ds(0, gs), :], 0.0).astype(jnp.bfloat16)

    if levels <= 8:
        for l in range(levels):
            amat[l] = upto(l)

    g_lane = lax.broadcasted_iota(jnp.int32, (BANDS, gs), 1)
    g_band = lax.broadcasted_iota(jnp.int32, (BANDS, gs), 0) * GPB
    inside = (g_lane >= g_band) & (g_lane < g_band + GPB)
    s_hi, s_lo = split(jnp.where(inside, pf_ref[...] * (1.0 / GPB), 0.0))
    smat[pl.ds(0, BANDS), :] = s_hi.astype(jnp.bfloat16)
    smat[pl.ds(BANDS, BANDS), :] = s_lo.astype(jnp.bfloat16)

    pl.semaphore_wait(barrier, n - 1)

    def send(i, carry):
        peer = partner(i)
        ps = div(peer, n_disk)
        pltpu.make_async_remote_copy(
            src_ref=pk.at[ps],
            dst_ref=recv.at[me],
            send_sem=send_sem,
            recv_sem=recv_sem,
            device_id=(ps, rem(peer, n_disk)),
            device_id_type=MESH,
        ).start()
        return carry

    lax.fori_loop(0, n - 1, send, 0)
    recv[me] = pk[me_s]

    src = src_ref[...]
    place = div(src, sector_cols) * block_cols + rem(src, block_cols)
    w = w_ref[...]
    taps, pixels = w.shape
    row = lax.broadcasted_iota(jnp.int32, (block_cols, pixels), 0)
    for d in range(n_disk):
        acc = None
        for k in range(taps):
            term = jnp.where(row + d * block_cols == place[k:k + 1, :], w[k:k + 1, :], 0.0)
            acc = term if acc is None else acc + term
        hi, lo = split(acc)
        hi = hi.astype(jnp.bfloat16)
        lo = lo.astype(jnp.bfloat16)
        for h in range(2):
            at = pl.ds((2 * d + h) * block_cols, block_cols)
            whi[at, :] = hi
            wlo[at, :] = lo

    arrive = pltpu.make_async_remote_copy(
        src_ref=recv.at[pl.ds(0, n - 1)], dst_ref=recv.at[pl.ds(0, n - 1)],
        send_sem=send_sem, recv_sem=recv_sem, device_id=(me_s, me_d), device_id_type=MESH,
    )
    arrive.wait_recv()

    left = lax.broadcasted_iota(jnp.int32, (2, LANES), 1) < 2 * block_cols
    for pair in range(n_disk // 2):
        cols = pl.ds(pair * LANES, LANES)
        for l in range(levels):
            even = recv[l * n_disk + 2 * pair]
            odds = recv[l * n_disk + 2 * pair + 1]
            x = jnp.where(left, even, odds)
            bmat[pl.ds(l, 1), cols] = x[0:1, :]
            fmat[pl.ds(levels + l, 1), cols] = x[1:2, :]
            zmat[pl.ds(l, 1), :] = jnp.where(left[0:1], odds[0:1], even[0:1])
        fmat[pl.ds(0, levels), cols] = pltpu.roll(zmat[...], LANES // 2, 1)
    f_hi, f_lo = split(fmat[...])
    fields = jnp.concatenate([f_hi, f_hi, f_lo], axis=0).astype(jnp.bfloat16)

    def step(l, a, carry):
        seen, emitted = carry
        onward = jnp.exp2(jnp.dot(a, fields, preferred_element_type=jnp.float32))
        return onward, emitted + bmat[pl.ds(l, 1), :] * (seen - onward)

    shape = (gs, fields.shape[1])
    carry = (jnp.ones(shape, jnp.float32), jnp.zeros(shape, jnp.float32))
    if levels <= 8:
        for l in range(levels):
            carry = step(l, amat[l], carry)
    else:
        carry = lax.fori_loop(0, levels, lambda l, c: step(l, upto(l), c), carry)
    e_hi, e_lo = split(carry[1] + bmat[pl.ds(levels - 1, 1), :] * carry[0])
    both = jnp.dot(smat[...], e_hi.astype(jnp.bfloat16), preferred_element_type=jnp.float32)
    rad = both[:BANDS] + both[BANDS:] + jnp.dot(
        smat[pl.ds(0, BANDS), :], e_lo.astype(jnp.bfloat16), preferred_element_type=jnp.float32
    )

    hour = (lax.broadcasted_iota(jnp.int32, rad.shape, 1) & block_cols) != 0
    lhs = jnp.concatenate([jnp.where(hour, 0.0, rad), jnp.where(hour, rad, 0.0)], axis=0)
    lhs = lhs.astype(jnp.bfloat16)
    res = jnp.dot(lhs, whi[...], preferred_element_type=jnp.float32) + jnp.dot(
        lhs, wlo[...], preferred_element_type=jnp.float32
    )
    out_ref[0] = res[:BANDS]
    out_ref[1] = res[BANDS:]
    arrive.wait_send()


def local(n_slab, n_disk, t, q, c, o, mol, cond, pf, src, w):
    hours, _, sector_cols = t.shape
    block_cols = sector_cols // n_slab
    taps, pixels = w.shape
    levels = mol.shape[1]
    n = n_slab * n_disk
    f32, bf16 = jnp.float32, jnp.bfloat16
    halves = sector_cols // LANES
    assert hours == 2 and n_disk * block_cols == LANES and n_disk == 4
    cond = cond.reshape(1, -1)
    pf = pf.reshape(1, -1)
    gs = BANDS * GPB
    kept = levels if levels <= 8 else 1
    args = (t, q, c, o, mol, cond, pf, src, w)
    vmem = pltpu.VMEM
    return pl.pallas_call(
        functools.partial(kernel, n_slab, n_disk, sector_cols, block_cols),
        out_shape=jax.ShapeDtypeStruct((hours, BANDS, pixels), f32),
        in_specs=[pl.BlockSpec(memory_space=pltpu.VMEM)] * len(args),
        out_specs=pl.BlockSpec(memory_space=pltpu.VMEM),
        scratch_shapes=[
            vmem((hours, 4 * halves, LANES), f32),
            vmem((n_slab, 2, LANES), f32),
            vmem((n, 2, LANES), f32),
            vmem((6 * levels, LANES), f32),
            vmem((LANES, 6 * levels), f32),
            vmem((kept, gs, 6 * levels), bf16),
            vmem((2 * levels, 2 * LANES), f32),
            vmem((levels, LANES), f32),
            vmem((levels, 2 * LANES), f32),
            vmem((2 * BANDS, gs), bf16),
            vmem((2 * LANES, pixels), bf16),
            vmem((2 * LANES, pixels), bf16),
            pltpu.SemaphoreType.DMA,
            pltpu.SemaphoreType.DMA,
        ],
        compiler_params=pltpu.CompilerParams(
            collective_id=0, has_side_effects=True, vmem_limit_bytes=32 * 1024 * 1024
        ),
    )(*args)


def solution(mesh):
    in_specs = (
        P(None, "slab", "disk"),
        P(None, "slab", "disk"),
        P(None, "slab", "disk"),
        P(None, "disk"),
        P(),
        P(),
        P(),
        P(None, ("slab", "disk")),
        P(None, ("slab", "disk")),
    )
    out_specs = P(None, None, ("slab", "disk"))
    fn = functools.partial(local, mesh.shape["slab"], mesh.shape["disk"])
    return jax.shard_map(fn, mesh=mesh, in_specs=in_specs, out_specs=out_specs, check_vma=False)
```

profile of v0, /device:TPU:0, one launch (start us, length us, event | category | flops | bytes accessed | tf_op | source)
XLA Modules:
  0.0 12.0 jit_solution(8611531657322165541)
XLA Ops:
  0.0 0.0 copy-start
  0.0 0.0 copy-start.1
  0.0 0.0 copy-start.2
  0.0 0.0 copy-start.3
  0.0 0.0 copy-start.4
  0.0 0.0 copy-start.5
  0.0 0.0 copy-start.6
  0.0 0.0 copy-start.7
  0.0 0.9 %copy.10.mol_ref = f32[112,8]{1,0:T(8,128)S(1)} copy(f32[112,8]{0,1:T(8,128)} %param.13) | data formatting | bytes 7168 | tf_op args[4]
  0.9 0.0 copy-done
  0.9 0.0 copy-done.1
  0.9 0.0 copy-done.2
  0.9 0.0 copy-done.3
  0.9 0.0 copy-done.4
  1.0 0.0 copy-done.5
  1.0 0.0 copy-done.6
  1.0 0.0 copy-done.7
  1.0 10.4 %shard_map.91 = f32[2,16,512]{2,1,0:T(8,128)S(1)} custom-call(f32[2,1,256]{2,1,0:T(1,128)S(1)} %copy-done.2, f32[2,1,256]{2,1,0:T(1,128)S(1)} %copy-done.3, f32[2,1,256]{2,1,0:T(1,128)S(1)} %copy-done.4, s32[2,256]{1,0:T(2,128)S(1)} %copy-done.5, f32[112,8]{1,0:T(8,128)S(1)} %copy.10.mol_ref, f32[1,112]{1,0:T(1,128)S(1)} %bitcast.2, f32[1,112]{1,0:T(1,128)S(1)} %bitcast.3, ...), custom_call_target="tpu_custom_call" | custom-call | tf_op jit(solution)/shard_map/pallas_call | solution.py:208
  11.4 0.6 %copy.12 = f32[2,16,512]{2,1,0:T(8,128)} copy(f32[2,16,512]{2,1,0:T(8,128)S(1)} %shard_map.91) | data formatting | bytes 131072
Async XLA Ops:
  0.0 0.9 %copy-start = (s32[4,512]{1,0:T(4,128)S(1)}, s32[4,512]{1,0:T(4,128)}, u32[]{:S(2)}) copy-start(s32[4,512]{1,0:T(4,128)} %src_ref.1) | copy-start | bytes 24580
  0.0 0.9 %copy-start.1 = (f32[4,512]{1,0:T(4,128)S(1)}, f32[4,512]{1,0:T(4,128)}, u32[]{:S(2)}) copy-start(f32[4,512]{1,0:T(4,128)} %w_ref.1) | copy-start | bytes 24580
  0.0 0.9 %copy-start.2 = (f32[2,1,256]{2,1,0:T(1,128)S(1)}, f32[2,1,256]{2,1,0:T(1,128)}, u32[]{:S(2)}) copy-start(f32[2,1,256]{2,1,0:T(1,128)} %t_ref.1) | copy-start | bytes 6148
  0.0 0.9 %copy-start.3 = (f32[2,1,256]{2,1,0:T(1,128)S(1)}, f32[2,1,256]{2,1,0:T(1,128)}, u32[]{:S(2)}) copy-start(f32[2,1,256]{2,1,0:T(1,128)} %q_ref.1) | copy-start | bytes 6148
  0.0 0.9 %copy-start.4 = (f32[2,1,256]{2,1,0:T(1,128)S(1)}, f32[2,1,256]{2,1,0:T(1,128)}, u32[]{:S(2)}) copy-start(f32[2,1,256]{2,1,0:T(1,128)} %c_ref.1) | copy-start | bytes 6148
  0.0 0.9 %copy-start.5 = (s32[2,256]{1,0:T(2,128)S(1)}, s32[2,256]{1,0:T(2,128)}, u32[]{:S(2)}) copy-start(s32[2,256]{1,0:T(2,128)} %o_ref.1) | copy-start | bytes 6148
  0.0 0.9 %copy-start.6 = (f32[112]{0:T(128)S(1)}, f32[112]{0:T(128)}, u32[]{:S(2)}) copy-start(f32[112]{0:T(128)} %param.14) | copy-start | bytes 1348
  0.0 0.9 %copy-start.7 = (f32[112]{0:T(128)S(1)}, f32[112]{0:T(128)}, u32[]{:S(2)}) copy-start(f32[112]{0:T(128)} %param.15) | copy-start | bytes 1348
where the time goes:
time: 12.1 us; the launch traced here: 12 us
  Pallas kernels  10.4 us (86%)
  local copies, waits for them, and re-layouts  1.53 us (13%)
    pallas_call x1, Pallas kernels, local(): pl.pallas_call(functools.partial(kernel, n_slab, n_disk, sector_cols, blo...  10.4 us
    unnamed x18, local copies, waits for them, and re-layouts  1.53 us

commit v1 on v0

--- a/solution.py
+++ b/solution.py
@@ -31,7 +31,7 @@
     n_slab, n_disk, sector_cols, block_cols,
     t_ref, q_ref, c_ref, o_ref, mol_ref, cond_ref, pf_ref, src_ref, w_ref,
     out_ref,
-    fld, pk, recv, cmat, mmat, amat, fmat, zmat, bmat, smat, whi, wlo,
+    fld, pk, recv, mmat, amat, fmat, zmat, bmat, smat, whi, wlo,
     send_sem, recv_sem,
 ):
     n = n_slab * n_disk
@@ -44,7 +44,7 @@
     me = me_s * n_disk + me_d
 
     def partner(i):
-        return me ^ (n - 1 - i) if n & (n - 1) == 0 else rem(me + (i + 1), n)
+        return rem(me + (i + 1), n)
 
     barrier = pltpu.get_barrier_semaphore()
 
@@ -83,12 +83,18 @@
         for k in range(halves):
             pk[k * per + s] = p[2 * k:2 * k + 2, :]
 
-    mol_hi, mol_lo = split(jnp.transpose(mol_ref[...]) * NEG_LOG2E)
-    cond_hi, cond_lo = split(cond_ref[...] * NEG_LOG2E)
-    cmat[...] = jnp.zeros_like(cmat)
-    for at, part in enumerate((mol_hi, cond_hi, mol_lo, cond_lo, mol_hi, cond_hi)):
-        cmat[pl.ds(at * levels, levels), pl.ds(0, gs)] = jnp.broadcast_to(part, (levels, gs))
-    mmat[...] = jnp.transpose(cmat[...])
+    g_lane = lax.broadcasted_iota(jnp.int32, (BANDS, gs), 1)
+    g_band = lax.broadcasted_iota(jnp.int32, (BANDS, gs), 0) * GPB
+    for j in range(GPB):
+        at = pl.ds(j * BANDS, BANDS)
+        hit = g_lane == g_band + j
+        cond = jnp.sum(jnp.where(hit, cond_ref[...], 0.0), axis=1, keepdims=True) * NEG_LOG2E
+        mol_hi, mol_lo = split(mol_ref[pl.ds(j, BANDS, stride=GPB), :] * NEG_LOG2E)
+        cond_hi, cond_lo = split(jnp.broadcast_to(cond, (BANDS, levels)))
+        for k, part in enumerate((mol_hi, cond_hi, mol_lo, cond_lo, mol_hi, cond_hi)):
+            mmat[at, pl.ds(k * levels, levels)] = part
+        pf = jnp.sum(jnp.where(hit, pf_ref[...], 0.0), axis=1, keepdims=True) * (1.0 / GPB)
+        smat[at, :] = jnp.broadcast_to(pf, (BANDS, LANES))
     col = rem(lax.broadcasted_iota(jnp.int32, (gs, 6 * levels), 1), levels)
 
     def upto(l):
@@ -97,13 +103,6 @@
     if levels <= 8:
         for l in range(levels):
             amat[l] = upto(l)
-
-    g_lane = lax.broadcasted_iota(jnp.int32, (BANDS, gs), 1)
-    g_band = lax.broadcasted_iota(jnp.int32, (BANDS, gs), 0) * GPB
-    inside = (g_lane >= g_band) & (g_lane < g_band + GPB)
-    s_hi, s_lo = split(jnp.where(inside, pf_ref[...] * (1.0 / GPB), 0.0))
-    smat[pl.ds(0, BANDS), :] = s_hi.astype(jnp.bfloat16)
-    smat[pl.ds(BANDS, BANDS), :] = s_lo.astype(jnp.bfloat16)
 
     pl.semaphore_wait(barrier, n - 1)
 
@@ -173,11 +172,13 @@
             carry = step(l, amat[l], carry)
     else:
         carry = lax.fori_loop(0, levels, lambda l, c: step(l, upto(l), c), carry)
-    e_hi, e_lo = split(carry[1] + bmat[pl.ds(levels - 1, 1), :] * carry[0])
-    both = jnp.dot(smat[...], e_hi.astype(jnp.bfloat16), preferred_element_type=jnp.float32)
-    rad = both[:BANDS] + both[BANDS:] + jnp.dot(
-        smat[pl.ds(0, BANDS), :], e_lo.astype(jnp.bfloat16), preferred_element_type=jnp.float32
-    )
+    glow = carry[1] + bmat[pl.ds(levels - 1, 1), :] * carry[0]
+    rad = None
+    for j in range(GPB):
+        at = slice(j * BANDS, (j + 1) * BANDS)
+        weight = smat[pl.ds(j * BANDS, BANDS), :]
+        term = jnp.concatenate([weight, weight], axis=1) * glow[at]
+        rad = term if rad is None else rad + term
 
     hour = (lax.broadcasted_iota(jnp.int32, rad.shape, 1) & block_cols) != 0
     lhs = jnp.concatenate([jnp.where(hour, 0.0, rad), jnp.where(hour, rad, 0.0)], axis=0)
@@ -214,13 +215,12 @@
             vmem((hours, 4 * halves, LANES), f32),
             vmem((n_slab, 2, LANES), f32),
             vmem((n, 2, LANES), f32),
-            vmem((6 * levels, LANES), f32),
-            vmem((LANES, 6 * levels), f32),
+            vmem((gs, 6 * levels), f32),
             vmem((kept, gs, 6 * levels), bf16),
             vmem((2 * levels, 2 * LANES), f32),
             vmem((levels, LANES), f32),
             vmem((levels, 2 * LANES), f32),
-            vmem((2 * BANDS, gs), bf16),
+            vmem((gs, LANES), f32),
             vmem((2 * LANES, pixels), bf16),
             vmem((2 * LANES, pixels), bf16),
             pltpu.SemaphoreType.DMA,

time: 12.1 us -> 11.7 us (0.967)
  Pallas kernels: 10.4 us -> 9.96 us
    pallas_call x1, Pallas kernels: 10.4 us -> 9.96 us  [local(): pl.pallas_call(functools.partial(kernel, n_slab, n_disk, sector_cols, blo...]
where the time goes in v1:
time: 11.7 us; the launch traced here: 11.6 us
  Pallas kernels  9.96 us (85%)
  local copies, waits for them, and re-layouts  1.53 us (13%)
    pallas_call x1, Pallas kernels, local(): pl.pallas_call(functools.partial(kernel, n_slab, n_disk, sector_cols, blo...  9.96 us
    unnamed x18, local copies, waits for them, and re-layouts  1.53 us

profile of v1, /device:TPU:0, one launch (start us, length us, event | category | flops | bytes accessed | tf_op | source)
XLA Modules:
  0.0 11.6 jit_solution(2758619123509533394)
XLA Ops:
  0.0 0.0 copy-start
  0.0 0.0 copy-start.1
  0.0 0.0 copy-start.2
  0.0 0.0 copy-start.3
  0.0 0.0 copy-start.4
  0.0 0.0 copy-start.5
  0.0 0.0 copy-start.6
  0.0 0.0 copy-start.7
  0.0 0.9 %copy.10.mol_ref = f32[112,8]{1,0:T(8,128)S(1)} copy(f32[112,8]{0,1:T(8,128)} %param.13) | data formatting | bytes 7168 | tf_op args[4]
  0.9 0.0 copy-done
  0.9 0.0 copy-done.1
  0.9 0.0 copy-done.2
  0.9 0.0 copy-done.3
  0.9 0.0 copy-done.4
  1.0 0.0 copy-done.5
  1.0 0.0 copy-done.6
  1.0 0.0 copy-done.7
  1.0 10.0 %shard_map.91 = f32[2,16,512]{2,1,0:T(8,128)S(1)} custom-call(f32[2,1,256]{2,1,0:T(1,128)S(1)} %copy-done.2, f32[2,1,256]{2,1,0:T(1,128)S(1)} %copy-done.3, f32[2,1,256]{2,1,0:T(1,128)S(1)} %copy-done.4, s32[2,256]{1,0:T(2,128)S(1)} %copy-done.5, f32[112,8]{1,0:T(8,128)S(1)} %copy.10.mol_ref, f32[1,112]{1,0:T(1,128)S(1)} %bitcast.2, f32[1,112]{1,0:T(1,128)S(1)} %bitcast.3, ...), custom_call_target="tpu_custom_call" | custom-call | tf_op jit(solution)/shard_map/pallas_call | solution.py:209
  11.0 0.6 %copy.12 = f32[2,16,512]{2,1,0:T(8,128)} copy(f32[2,16,512]{2,1,0:T(8,128)S(1)} %shard_map.91) | data formatting | bytes 131072
Async XLA Ops:
  0.0 0.9 %copy-start = (s32[4,512]{1,0:T(4,128)S(1)}, s32[4,512]{1,0:T(4,128)}, u32[]{:S(2)}) copy-start(s32[4,512]{1,0:T(4,128)} %src_ref.1) | copy-start | bytes 24580
  0.0 0.9 %copy-start.1 = (f32[4,512]{1,0:T(4,128)S(1)}, f32[4,512]{1,0:T(4,128)}, u32[]{:S(2)}) copy-start(f32[4,512]{1,0:T(4,128)} %w_ref.1) | copy-start | bytes 24580
  0.0 0.9 %copy-start.2 = (f32[2,1,256]{2,1,0:T(1,128)S(1)}, f32[2,1,256]{2,1,0:T(1,128)}, u32[]{:S(2)}) copy-start(f32[2,1,256]{2,1,0:T(1,128)} %t_ref.1) | copy-start | bytes 6148
  0.0 0.9 %copy-start.3 = (f32[2,1,256]{2,1,0:T(1,128)S(1)}, f32[2,1,256]{2,1,0:T(1,128)}, u32[]{:S(2)}) copy-start(f32[2,1,256]{2,1,0:T(1,128)} %q_ref.1) | copy-start | bytes 6148
  0.0 0.9 %copy-start.4 = (f32[2,1,256]{2,1,0:T(1,128)S(1)}, f32[2,1,256]{2,1,0:T(1,128)}, u32[]{:S(2)}) copy-start(f32[2,1,256]{2,1,0:T(1,128)} %c_ref.1) | copy-start | bytes 6148
  0.0 0.9 %copy-start.5 = (s32[2,256]{1,0:T(2,128)S(1)}, s32[2,256]{1,0:T(2,128)}, u32[]{:S(2)}) copy-start(s32[2,256]{1,0:T(2,128)} %o_ref.1) | copy-start | bytes 6148
  0.0 0.9 %copy-start.6 = (f32[112]{0:T(128)S(1)}, f32[112]{0:T(128)}, u32[]{:S(2)}) copy-start(f32[112]{0:T(128)} %param.14) | copy-start | bytes 1348
  0.0 0.9 %copy-start.7 = (f32[112]{0:T(128)S(1)}, f32[112]{0:T(128)}, u32[]{:S(2)}) copy-start(f32[112]{0:T(128)} %param.15) | copy-start | bytes 1348

commit v2 on v1

--- a/solution.py
+++ b/solution.py
@@ -102,7 +102,7 @@
 
     if levels <= 8:
         for l in range(levels):
-            amat[l] = upto(l)
+            amat[pl.ds(l * gs, gs), :] = upto(l)
 
     pl.semaphore_wait(barrier, n - 1)
 
@@ -160,18 +160,19 @@
     f_hi, f_lo = split(fmat[...])
     fields = jnp.concatenate([f_hi, f_hi, f_lo], axis=0).astype(jnp.bfloat16)
 
-    def step(l, a, carry):
+    def step(l, depth, carry):
         seen, emitted = carry
-        onward = jnp.exp2(jnp.dot(a, fields, preferred_element_type=jnp.float32))
+        onward = jnp.exp2(depth)
         return onward, emitted + bmat[pl.ds(l, 1), :] * (seen - onward)
 
     shape = (gs, fields.shape[1])
     carry = (jnp.ones(shape, jnp.float32), jnp.zeros(shape, jnp.float32))
     if levels <= 8:
+        depths = jnp.dot(amat[...], fields, preferred_element_type=jnp.float32)
         for l in range(levels):
-            carry = step(l, amat[l], carry)
+            carry = step(l, depths[l * gs:(l + 1) * gs], carry)
     else:
-        carry = lax.fori_loop(0, levels, lambda l, c: step(l, upto(l), c), carry)
+        carry = lax.fori_loop(0, levels, lambda l, c: step(l, jnp.dot(upto(l), fields, preferred_element_type=jnp.float32), c), carry)
     glow = carry[1] + bmat[pl.ds(levels - 1, 1), :] * carry[0]
     rad = None
     for j in range(GPB):
@@ -216,7 +217,7 @@
             vmem((n_slab, 2, LANES), f32),
             vmem((n, 2, LANES), f32),
             vmem((gs, 6 * levels), f32),
-            vmem((kept, gs, 6 * levels), bf16),
+            vmem((kept * gs, 6 * levels), bf16),
             vmem((2 * levels, 2 * LANES), f32),
             vmem((levels, LANES), f32),
             vmem((levels, 2 * LANES), f32),

time: 11.7 us -> 11.8 us (level)
  Pallas kernels: 9.96 us -> 10.1 us
where the time goes in v2:
time: 11.8 us; the launch traced here: 11.7 us
  Pallas kernels  10.1 us (86%)
  local copies, waits for them, and re-layouts  1.53 us (13%)
    pallas_call x1, Pallas kernels, local(): pl.pallas_call(functools.partial(kernel, n_slab, n_disk, sector_cols, blo...  10.1 us
    unnamed x18, local copies, waits for them, and re-layouts  1.53 us

profile of v2, /device:TPU:0, one launch (start us, length us, event | category | flops | bytes accessed | tf_op | source)
XLA Modules:
  0.0 11.7 jit_solution(3747939458335949219)
XLA Ops:
  0.0 0.0 copy-start
  0.0 0.0 copy-start.1
  0.0 0.0 copy-start.2
  0.0 0.0 copy-start.3
  0.0 0.0 copy-start.4
  0.0 0.0 copy-start.5
  0.0 0.0 copy-start.6
  0.0 0.0 copy-start.7
  0.0 0.9 %copy.10.mol_ref = f32[112,8]{1,0:T(8,128)S(1)} copy(f32[112,8]{0,1:T(8,128)} %param.13) | data formatting | bytes 7168 | tf_op args[4]
  0.9 0.0 copy-done
  0.9 0.0 copy-done.1
  0.9 0.0 copy-done.2
  0.9 0.0 copy-done.3
  0.9 0.0 copy-done.4
  1.0 0.0 copy-done.5
  1.0 0.0 copy-done.6
  1.0 0.0 copy-done.7
  1.0 10.1 %shard_map.91 = f32[2,16,512]{2,1,0:T(8,128)S(1)} custom-call(f32[2,1,256]{2,1,0:T(1,128)S(1)} %copy-done.2, f32[2,1,256]{2,1,0:T(1,128)S(1)} %copy-done.3, f32[2,1,256]{2,1,0:T(1,128)S(1)} %copy-done.4, s32[2,256]{1,0:T(2,128)S(1)} %copy-done.5, f32[112,8]{1,0:T(8,128)S(1)} %copy.10.mol_ref, f32[1,112]{1,0:T(1,128)S(1)} %bitcast.2, f32[1,112]{1,0:T(1,128)S(1)} %bitcast.3, ...), custom_call_target="tpu_custom_call" | custom-call | tf_op jit(solution)/shard_map/pallas_call | solution.py:210
  11.1 0.6 %copy.12 = f32[2,16,512]{2,1,0:T(8,128)} copy(f32[2,16,512]{2,1,0:T(8,128)S(1)} %shard_map.91) | data formatting | bytes 131072
Async XLA Ops:
  0.0 0.9 %copy-start = (s32[4,512]{1,0:T(4,128)S(1)}, s32[4,512]{1,0:T(4,128)}, u32[]{:S(2)}) copy-start(s32[4,512]{1,0:T(4,128)} %src_ref.1) | copy-start | bytes 24580
  0.0 0.9 %copy-start.1 = (f32[4,512]{1,0:T(4,128)S(1)}, f32[4,512]{1,0:T(4,128)}, u32[]{:S(2)}) copy-start(f32[4,512]{1,0:T(4,128)} %w_ref.1) | copy-start | bytes 24580
  0.0 0.9 %copy-start.2 = (f32[2,1,256]{2,1,0:T(1,128)S(1)}, f32[2,1,256]{2,1,0:T(1,128)}, u32[]{:S(2)}) copy-start(f32[2,1,256]{2,1,0:T(1,128)} %t_ref.1) | copy-start | bytes 6148
  0.0 0.9 %copy-start.3 = (f32[2,1,256]{2,1,0:T(1,128)S(1)}, f32[2,1,256]{2,1,0:T(1,128)}, u32[]{:S(2)}) copy-start(f32[2,1,256]{2,1,0:T(1,128)} %q_ref.1) | copy-start | bytes 6148
  0.0 0.9 %copy-start.4 = (f32[2,1,256]{2,1,0:T(1,128)S(1)}, f32[2,1,256]{2,1,0:T(1,128)}, u32[]{:S(2)}) copy-start(f32[2,1,256]{2,1,0:T(1,128)} %c_ref.1) | copy-start | bytes 6148
  0.0 0.9 %copy-start.5 = (s32[2,256]{1,0:T(2,128)S(1)}, s32[2,256]{1,0:T(2,128)}, u32[]{:S(2)}) copy-start(s32[2,256]{1,0:T(2,128)} %o_ref.1) | copy-start | bytes 6148
  0.0 0.9 %copy-start.6 = (f32[112]{0:T(128)S(1)}, f32[112]{0:T(128)}, u32[]{:S(2)}) copy-start(f32[112]{0:T(128)} %param.14) | copy-start | bytes 1348
  0.0 0.9 %copy-start.7 = (f32[112]{0:T(128)S(1)}, f32[112]{0:T(128)}, u32[]{:S(2)}) copy-start(f32[112]{0:T(128)} %param.15) | copy-start | bytes 1348
